TPU v7x, 128 devices: a whole 4x4x4 slice. The times are simulated.
128 devices in a mesh: blk: 4 (over y_hi, core), ga: 32 (over x, y_lo, z).
Axes of the slice: x: 4, y: 4 (y_hi: 2, y_lo: 2; y = y_hi * 2 + y_lo), z: 4, core: 2. Of those that a mesh axis runs over, the one named last changes fastest.
Arguments:
- screening: bfloat16 [16384, 16384], P('ga', 'blk'), as said below
- pair_elements: bfloat16 [16384, 2048], P('ga', 'blk'), may hold values from -6 to 6
- summed_bands: int32 [16], P('blk'), may hold values from 0 to 2047
- occupied: int32 [1], replicated, may hold values from 768 to 1280
Outputs:
- sigma: float32 [128, 128], P(('blk', 'ga'))
Inputs may be any that keep to these rules, and one draw needn't show every extreme that they name: screening is symmetric: screening[G, G'] = screening[G', G]; its diagonal lies between 0.3 and 3 and its off-diagonal entries have magnitude at most 4 / sqrt(16384).
All inputs are finite; a program needn't handle non-finite values.
Results may differ from a plain program's by a relative error of at most 0.0017.
Values may be sent and summed in bfloat16 or wider, within the bound.
No kernel may reach another device: no remote copies, remote signals or barrier semaphores. Data moves between devices by JAX's collectives and lax.ppermute only.
A program may use at most 128 MiB of HBM per device.

v0:
```python
import math

import jax
import jax.numpy as jnp
from jax import lax
from jax.experimental import pallas as pl
from jax.experimental.pallas import tpu as pltpu
from jax.sharding import PartitionSpec as P

NS = 128
AXES = ("blk", "ga")


def place(x, y, z, core):
    return ((y // 2) * 2 + core) * 32 + (x % 4) * 8 + (y % 2) * 4 + z % 4


def pairs(target, keep=lambda x, y, z, core: True):
    return [
        (place(x, y, z, core), place(*target(x, y, z, core)))
        for x in range(4)
        for y in range(4)
        for z in range(4)
        for core in range(2)
        if keep(x, y, z, core)
    ]


def inner(x, y):
    return x // 2 == y // 2


def far_core(x, y):
    return 1 - (x if inner(x, y) else 3 - x) % 2


def is_inner(x, y, z, core):
    return inner(x, y)


def is_far(x, y, z, core):
    return core == far_core(x, y)


def to_near_plane(x, y, z, core):
    return (3 - x, y, z, core) if inner(x, y) else (x, (y + 2) % 4, z, core)


def to_partner(x, y, z, core):
    return x ^ 1, y, z, far_core(x ^ 1, y)


CORE_NEAR = pairs(
    lambda x, y, z, core: (x, y, z, 1 - core), lambda x, y, z, core: not is_far(x, y, z, core)
)
CORE_FAR = pairs(lambda x, y, z, core: (x, y, z, 1 - core), is_far)
INJECT = pairs(to_near_plane)
RETURN = pairs(to_near_plane, lambda x, y, z, core: not inner(x, y))
SWAP = pairs(to_partner, is_far)
PARTNER = pairs(lambda x, y, z, core: (x ^ 1, y, z, core))
SIDE = pairs(lambda x, y, z, core: (x, y ^ 1, z, core))
SIDE_INNER = pairs(lambda x, y, z, core: (x, y ^ 1, z, core), is_inner)


def down(x, y, z, core):
    return x, y, z - 1, core


def up(x, y, z, core):
    return x, y, z + 1, core


DOWN, UP = pairs(down), pairs(up)

SLOTS = 9
NEAR, INNER, SIDE_OWN, ROLE = range(SLOTS, SLOTS + 4)


def send(value, table):
    return lax.ppermute(value, AXES, table)


def blend(flag, yes, no):
    flag = flag.astype(yes.dtype)
    return yes * flag + no * (1 - flag)


def products(table, factors, near, far, weight_b, blocks, before=None, scale=None):
    (near_w, *near_rows), (far_w, *far_rows) = near, far
    parts = [len(near_w), len(far_w)]
    rows, (depth, width) = sum(part.shape[0] for part in near_w), blocks[0].shape
    bands = width // NS

    def kernel(table, factors, *refs):
        near_refs, refs = refs[: parts[0]], refs[parts[0] :]
        far_refs, refs = refs[: parts[1]], refs[parts[1] :]
        near_a, *near_b = refs[:3]
        far_a, *far_b = refs[3:6]
        weight_ref, refs = refs[6], refs[7:]
        own, brought, own_side, brought_side, up_1, down_1, up_2, down_2 = refs[:8]
        across_up, across_down = refs[8:10]
        refs = refs[10:]
        if before is not None:
            before_ref, refs = refs[0], refs[1:]
        out, w, q, left, sems = refs

        def choose(flag, yes, no):
            if yes is no:
                copy(*yes)
                return

            @pl.when(table[flag] == 1)
            def _():
                copy(*yes)

            @pl.when(table[flag] == 0)
            def _():
                copy(*no)

        def copy(*triples):
            for source, target, sem in triples:
                pltpu.make_async_copy(source, target, sem).start()

        def part(slot):
            return slot // 4, pl.ds((slot % 4) * depth, depth)

        sources = [
            (INNER, own, brought),
            (INNER, up_1, up_1),
            (INNER, up_2, up_2),
            (INNER, across_up, across_up),
            (INNER, brought, brought),
            (INNER, down_1, down_1),
            (INNER, down_2, down_2),
            (INNER, across_down, across_down),
            (SIDE_OWN, own_side, brought_side),
        ]
        for slot in (8, 0, 1, 2, 3, 4, 5, 6, 7):
            flag, yes, no = sources[slot]
            yes, no = yes.at[pl.ds(0, depth)], no.at[pl.ds(0, depth)] if no is not yes else None
            group, place_in = part(slot)
            target, sem = q.at[group, place_in], sems.at[0, group]
            if no is None:
                copy((yes, target, sem))
            else:
                choose(flag, [(yes, target, sem)], [(no, target, sem)])
            columns = pl.ds(pl.multiple_of(table[slot] * depth, depth), depth)
            copies = []
            for side in (near_refs, far_refs):
                at, triples = 0, []
                for ref in side:
                    target = w.at[group, pl.ds(at, ref.shape[0]), place_in]
                    triples.append((ref.at[:, columns], target, sems.at[1, group]))
                    at += ref.shape[0]
                copies.append(triples)
            choose(NEAR, *copies)
        block = pl.ds(0, rows)
        target, sem = left.at[0], sems.at[0, 3]
        choose(NEAR, [(near_a.at[block], target, sem)], [(far_a.at[block], target, sem)])
        target, sem = left.at[1], sems.at[1, 3]
        for role, source in enumerate((far_b[1], far_b[0], near_b[1], near_b[0])):

            @pl.when(table[ROLE] == role)
            def _(source=source):
                copy((source.at[block], target, sem))

        def wait(ref, sem):
            pltpu.make_async_copy(ref, ref, sem).wait()

        wait(q.at[2, pl.ds(0, depth)], sems.at[0, 2])
        wait(w.at[2, :, pl.ds(0, depth)], sems.at[1, 2])
        side = jnp.dot(w[2, :, :depth], q[2, :depth], preferred_element_type=jnp.float32)
        result = jnp.zeros((NS, 2 * NS), jnp.float32)
        for group in range(2):
            wait(q.at[group], sems.at[0, group])
            wait(w.at[group], sems.at[1, group])
            q[group, :depth] = q[group, :depth] * factors[group].astype(q.dtype)
            total = jnp.dot(w[group], q[group], preferred_element_type=jnp.float32)
            total = total + side * factors[2 + group]
            if group == 1:
                total = total * weight_ref[0:1, :].astype(jnp.float32)
            high = total.astype(jnp.bfloat16)
            low = (total - high.astype(jnp.float32)).astype(jnp.bfloat16)
            wait(left.at[group], sems.at[group, 3])
            for band in range(bands):
                lanes = slice(band * NS, (band + 1) * NS)
                result = result + lax.dot_general(
                    left[group, :, lanes],
                    jnp.concatenate([high[:, lanes], low[:, lanes]], 1),
                    (((0,), (0,)), ((), ())),
                    preferred_element_type=jnp.float32,
                )
        result = result[:, :NS] + result[:, NS:]
        if before is not None:
            result = result + before_ref[...]
            result = (result + result.T) * jnp.float32(scale)
        out[...] = result

    hbm = pl.BlockSpec(memory_space=pl.ANY)
    vmem = pl.BlockSpec(memory_space=pltpu.VMEM)
    smem = pl.BlockSpec(memory_space=pltpu.SMEM)
    more = [] if before is None else [before]
    return pl.pallas_call(
        kernel,
        out_shape=jax.ShapeDtypeStruct((NS, NS), jnp.float32),
        in_specs=[smem, smem] + [hbm] * (sum(parts) + 6) + [vmem] + [hbm] * 10 + [vmem] * len(more),
        out_specs=vmem,
        scratch_shapes=[
            pltpu.VMEM((3, rows, 4 * depth), jnp.bfloat16),
            pltpu.VMEM((3, 4 * depth, width), jnp.bfloat16),
            pltpu.VMEM((2, rows, width), jnp.bfloat16),
            pltpu.SemaphoreType.DMA((2, 4)),
        ],
        compiler_params=pltpu.CompilerParams(vmem_limit_bytes=63 * 1024 * 1024),
        cost_estimate=pl.CostEstimate(
            flops=2 * SLOTS * rows * depth * width,
            bytes_accessed=2 * SLOTS * (rows + width) * depth,
            transcendentals=0,
        ),
    )(table, factors, *near_w, *far_w, *near_rows, *far_rows, weight_b, *blocks, *more)


def shards(screening, pair_elements, summed_bands, occupied):
    rows = pair_elements.shape[0]
    bands = summed_bands.shape[0]
    total_g = rows * lax.axis_size("ga")
    scale = 1.0 / math.sqrt(total_g * bands * lax.axis_size("blk"))
    blk, ga = lax.axis_index("blk"), lax.axis_index("ga")
    y_hi, core = blk // 2, blk % 2
    x, y_lo, z = ga // 8, (ga // 4) % 2, ga % 4
    at_inner = x // 2 == y_hi
    near_plane = jnp.where(at_inner, x, 3 - x)
    near = core == near_plane % 2

    low, first = z < 2, y_lo == 0
    other = 1 - y_lo
    z_up, z_down, z_across = (z + 1) % 4, (z + 3) % 4, (z + 2) % 4
    table = [y_lo * 4 + z, y_lo * 4 + z_up, other * 4 + z_up]
    table += [jnp.where(low, y_lo, other) * 4 + z_across]
    table += [y_lo * 4 + z, y_lo * 4 + z_down, other * 4 + z_down]
    table += [jnp.where(low, other, y_lo) * 4 + z_across, other * 4 + z]
    table += [near, at_inner, at_inner & first, near * 2 + at_inner]
    table = jnp.stack([entry.astype(jnp.int32) for entry in table])
    odd = x % 2
    sides = [first, ~first]
    factors_own = [jnp.where(at_inner, 0.5, 1.0), jnp.where(at_inner, 0.5, 0.0)] + sides
    factors_partner = [jnp.where(at_inner, odd, 1), jnp.where(at_inner, 1 - odd, 0)] + sides
    factors_own = jnp.stack([entry * jnp.float32(1) for entry in factors_own])
    factors_partner = jnp.stack([entry * jnp.float32(1) for entry in factors_partner])
    factors_here = jnp.where(near, factors_own, factors_partner)
    factors_there = jnp.where(near, factors_partner, factors_own)
    one = jnp.ones((1, bands * NS), pair_elements.dtype)
    weight = jnp.where(summed_bands < occupied[0], -0.5, 0.5).astype(pair_elements.dtype)
    weight = jnp.broadcast_to(jnp.repeat(weight, NS)[None, :], (16, bands * NS))

    held = lax.optimization_barrier
    own = pair_elements
    cut = rows * 11 // 16
    brought = send(jnp.concatenate([own, weight], 0), INJECT)
    own_side = send(own, SIDE_INNER)
    own_rows = own * weight[:1]
    partner_rows = send(own_rows, PARTNER)
    (
        near_w, brought, own_side, partner_rows, own_rows, far_1, far_2,
        table, factors_here, factors_there, one,
    ) = held(
        (
            screening, brought, own_side, partner_rows, own_rows, screening[:cut], screening[cut:],
            table, factors_here, factors_there, one,
        )
    )

    swapped_1 = send(far_1, SWAP)
    brought_side = send(brought, SIDE)
    up_1 = send(blend(at_inner, own, brought[:rows]), DOWN)
    down_1 = send(brought, UP)
    native_side = blend(at_inner, own_side, brought_side[:rows])
    own_side, brought, brought_side, native_side, up_1, down_1, partner_rows, near_w = held(
        (own_side, brought, brought_side, native_side, up_1, down_1, partner_rows, near_w)
    )

    up_2 = send(native_side, DOWN)
    down_2 = send(brought_side, UP)
    brought_weight = jnp.where(at_inner, brought[rows : rows + 1], one)
    weight_here = jnp.where(near, brought_weight, one)
    weight_there = jnp.where(near, one, brought_weight)
    foreign_rows = send(partner_rows, RETURN)
    swapped_1, foreign_rows, up_1, down_1, up_2, down_2, far_2, weight_here, weight_there, near_w = held(
        (swapped_1, foreign_rows, up_1, down_1, up_2, down_2, far_2, weight_here, weight_there, near_w)
    )

    swapped_2 = send(far_2, SWAP)
    across_up = send(blend((z + 3) % 4 < 2, up_1, up_2), DOWN)
    across_down = send(blend((z + 1) % 4 < 2, down_2, down_1), UP)
    near_other = send(near_w, CORE_NEAR)
    swapped_1, swapped_2, across_up, across_down, foreign_rows, near_other = held(
        (swapped_1, swapped_2, across_up, across_down, foreign_rows, near_other)
    )

    swapped_other = [send(swapped_1, CORE_FAR), send(swapped_2, CORE_FAR)]
    blocks = [own, brought, own_side, brought_side, up_1, down_1, up_2, down_2]
    blocks += [across_up, across_down]
    half = products(
        table,
        factors_here,
        ([screening], own_rows, brought, own_rows),
        ([swapped_1, swapped_2], partner_rows, foreign_rows, partner_rows),
        weight_here,
        blocks,
    )
    value = products(
        table,
        factors_there,
        (swapped_other, partner_rows, foreign_rows, partner_rows),
        ([near_other], own_rows, brought, own_rows),
        weight_there,
        blocks,
        half,
        scale,
    )
    parts = lax.all_to_all(value.reshape(NS, 1, NS), AXES, 0, 0)
    return jnp.sum(parts, 0)


def solution(mesh):
    placed = (P("ga", "blk"), P("ga", "blk"), P("blk"), P())
    return jax.shard_map(
        shards, mesh=mesh, in_specs=placed, out_specs=P(("blk", "ga"), None), check_vma=False
    )
```

profile of v0, /device:TPU:1, one launch (start us, length us, event | category | flops | bytes accessed | tf_op | source)
XLA Modules:
  0.0 120.3 jit_solution(4703773657181134338)
XLA Ops:
  1.5 1.9 %pad_maximum_fusion = bf16[528,512]{1,0:T(8,128)(2,1)} fusion(bf16[16,512]{1,0:T(8,128)(2,1)S(1)} %broadcast_in_dim.25, bf16[512,512]{1,0:T(8,128)(2,1)} %refs_10_.3), kind=kLoop, calls=%fused_computation | loop fusion | flops 1081344 | bytes 1081344 | tf_op jit(solution)/shard_map/concatenate | solution.py:259
  3.3 3.3 %collective-permute-start = (bf16[528,512]{1,0:T(8,128)(2,1)}, bf16[528,512]{1,0:T(8,128)(2,1)S(1)}, u32[]{:S(2)}, u32[]{:S(2)}) collective-permute-start(bf16[528,512]{1,0:T(8,128)(2,1)} %pad_maximum_fusion), channel_id=1, source_target_pairs={{0,24},{32,56},{1,25},{33,57},{2,26},{34,58},{3,27},{35,59},{4,28}... | collective-permute-start | bytes 1622024 | tf_op jit(solution)/shard_map/ppermute | solution.py:80
  6.8 3.2 %collective-permute-start.1 = (bf16[512,512]{1,0:T(8,128)(2,1)S(1)}, bf16[512,512]{1,0:T(8,128)(2,1)S(1)}, u32[]{:S(2)}, u32[]{:S(2)}) collective-permute-start(bf16[512,512]{1,0:T(8,128)(2,1)S(1)} %copy-done.2), channel_id=1, source_target_pairs={{0,4},{32,36},{1,5},{33,37},{2,6},{34,38},{3,7},{35,39},{4,0},{36,... | collective-permute-start | bytes 1572872 | tf_op jit(solution)/shard_map/ppermute | solution.py:80
  10.2 2.5 %slice.17 = bf16[160,4096]{1,0:T(8,128)(2,1)} slice(bf16[512,4096]{1,0:T(8,128)(2,1)} %refs_0_.1), slice={[352:512], [0:4096]} | slice | bytes 2621440 | tf_op jit(solution)/shard_map/slice | solution.py:268
  12.7 3.7 %slice.16 = bf16[352,4096]{1,0:T(8,128)(2,1)} slice(bf16[512,4096]{1,0:T(8,128)(2,1)} %refs_0_.1), slice={[0:352], [0:4096]} | slice | bytes 5767168 | tf_op jit(solution)/shard_map/slice | solution.py:268
  19.3 1.7 %collective-permute-done.1.refs_12_ = bf16[512,512]{1,0:T(8,128)(2,1)S(1)} collective-permute-done((bf16[512,512]{1,0:T(8,128)(2,1)S(1)}, bf16[512,512]{1,0:T(8,128)(2,1)S(1)}, u32[]{:S(2)}, u32[]{:S(2)}) %collective-permute-start.1) | collective-permute-done | bytes 524320 | tf_op jit(solution)/shard_map/ppermute | solution.py:80
  21.0 5.3 %collective-permute-start.3 = (bf16[352,4096]{1,0:T(8,128)(2,1)}, bf16[352,4096]{1,0:T(8,128)(2,1)}, u32[]{:S(2)}, u32[]{:S(2)}) collective-permute-start(bf16[352,4096]{1,0:T(8,128)(2,1)} %slice.16), channel_id=1, source_target_pairs={{32,8},{33,9},{34,10},{35,11},{36,12},{37,13},{38,14},{39,15},{64,... | collective-permute-start | bytes 8650760 | tf_op jit(solution)/shard_map/ppermute | solution.py:80
  27.7 1.6 %collective-permute-start.6 = (bf16[528,512]{1,0:T(8,128)(2,1)S(1)}, bf16[528,512]{1,0:T(8,128)(2,1)S(1)}, u32[]{:S(2)}, u32[]{:S(2)}) collective-permute-start(bf16[528,512]{1,0:T(8,128)(2,1)S(1)} %collective-permute-done.refs_4_.refs_11_.refs_7_), channel_id=1, source_target_pairs={{0,1},{32,33},{1,2},{33,34},{2,3},{34,35},{3,0},{35,32},{4,5},{36,... | collective-permute-start | bytes 1622024 | tf_op jit(solution)/shard_map/ppermute | solution.py:80
  29.4 2.2 %collective-permute-start.5 = (bf16[512,512]{1,0:T(8,128)(2,1)S(1)}, bf16[512,512]{1,0:T(8,128)(2,1)S(1)}, u32[]{:S(2)}, u32[]{:S(2)}) collective-permute-start(bf16[512,512]{1,0:T(8,128)(2,1)S(1)} %multiply_add_fusion.2), channel_id=1, source_target_pairs={{0,3},{32,35},{1,0},{33,32},{2,1},{34,33},{3,2},{35,34},{4,7},{36,... | collective-permute-start | bytes 1572872 | tf_op jit(solution)/shard_map/ppermute | solution.py:80
  31.6 8.5 %collective-permute-done.4.refs_13_ = bf16[528,512]{1,0:T(8,128)(2,1)} collective-permute-done((bf16[528,512]{1,0:T(8,128)(2,1)S(1)}, bf16[528,512]{1,0:T(8,128)(2,1)}, u32[]{:S(2)}, u32[]{:S(2)}) %collective-permute-start.4) | collective-permute-done | bytes 540704 | tf_op jit(solution)/shard_map/ppermute | solution.py:80
  41.2 2.0 %collective-permute-done.5.refs_14_ = bf16[512,512]{1,0:T(8,128)(2,1)S(1)} collective-permute-done((bf16[512,512]{1,0:T(8,128)(2,1)S(1)}, bf16[512,512]{1,0:T(8,128)(2,1)S(1)}, u32[]{:S(2)}, u32[]{:S(2)}) %collective-permute-start.5) | collective-permute-done | bytes 524320 | tf_op jit(solution)/shard_map/ppermute | solution.py:80
  43.4 1.7 %collective-permute-start.9 = (bf16[528,512]{1,0:T(8,128)(2,1)}, bf16[528,512]{1,0:T(8,128)(2,1)S(1)}, u32[]{:S(2)}, u32[]{:S(2)}) collective-permute-start(bf16[528,512]{1,0:T(8,128)(2,1)} %collective-permute-done.4.refs_13_), channel_id=1, source_target_pairs={{0,1},{32,33},{1,2},{33,34},{2,3},{34,35},{3,0},{35,32},{4,5},{36,... | collective-permute-start | bytes 1622024 | tf_op jit(solution)/shard_map/ppermute | solution.py:80
  48.2 9.6 %collective-permute-done.8.refs_16_ = bf16[512,512]{1,0:T(8,128)(2,1)S(1)} collective-permute-done((bf16[512,512]{1,0:T(8,128)(2,1)S(1)}, bf16[512,512]{1,0:T(8,128)(2,1)S(1)}, u32[]{:S(2)}, u32[]{:S(2)}) %collective-permute-start.8) | collective-permute-done | bytes 524320 | tf_op jit(solution)/shard_map/ppermute | solution.py:80
  57.9 4.6 %collective-permute-done.7.refs_7_.refs_4_ = bf16[512,512]{1,0:T(8,128)(2,1)S(1)} collective-permute-done((bf16[512,512]{1,0:T(8,128)(2,1)S(1)}, bf16[512,512]{1,0:T(8,128)(2,1)S(1)}, u32[]{:S(2)}, u32[]{:S(2)}) %collective-permute-start.7) | collective-permute-done | bytes 524320 | tf_op jit(solution)/shard_map/ppermute | solution.py:80
  63.3 1.4 %collective-permute-start.13 = (bf16[512,4096]{1,0:T(8,128)(2,1)}, bf16[512,4096]{1,0:T(8,128)(2,1)}, u32[]{:S(2)}, u32[]{:S(2)}) collective-permute-start(bf16[512,4096]{1,0:T(8,128)(2,1)} %refs_0_.1), channel_id=1, source_target_pairs={{0,32},{1,33},{2,34},{3,35},{4,36},{5,37},{6,38},{7,39},{96,64},{9... | collective-permute-start | bytes 12582920 | tf_op jit(solution)/shard_map/ppermute | solution.py:80
  64.7 1.9 %collective-permute-start.10 = (bf16[160,4096]{1,0:T(8,128)(2,1)}, bf16[160,4096]{1,0:T(8,128)(2,1)}, u32[]{:S(2)}, u32[]{:S(2)}) collective-permute-start(bf16[160,4096]{1,0:T(8,128)(2,1)} %slice.17), channel_id=1, source_target_pairs={{32,8},{33,9},{34,10},{35,11},{36,12},{37,13},{38,14},{39,15},{64,... | collective-permute-start | bytes 3932168 | tf_op jit(solution)/shard_map/ppermute | solution.py:80
  66.9 2.7 %collective-permute-start.11 = (bf16[512,512]{1,0:T(8,128)(2,1)S(1)}, bf16[512,512]{1,0:T(8,128)(2,1)S(1)}, u32[]{:S(2)}, u32[]{:S(2)}) collective-permute-start(bf16[512,512]{1,0:T(8,128)(2,1)S(1)} %multiply_add_fusion.1), channel_id=1, source_target_pairs={{0,3},{32,35},{1,0},{33,32},{2,1},{34,33},{3,2},{35,34},{4,7},{36,... | collective-permute-start | bytes 1572872 | tf_op jit(solution)/shard_map/ppermute | solution.py:80
  69.7 7.6 %collective-permute-done.11.refs_18_ = bf16[512,512]{1,0:T(8,128)(2,1)S(1)} collective-permute-done((bf16[512,512]{1,0:T(8,128)(2,1)S(1)}, bf16[512,512]{1,0:T(8,128)(2,1)S(1)}, u32[]{:S(2)}, u32[]{:S(2)}) %collective-permute-start.11) | collective-permute-done | bytes 524320 | tf_op jit(solution)/shard_map/ppermute | solution.py:80
  78.6 5.3 %collective-permute-done.10.refs_2_ = bf16[160,4096]{1,0:T(8,128)(2,1)} collective-permute-done((bf16[160,4096]{1,0:T(8,128)(2,1)}, bf16[160,4096]{1,0:T(8,128)(2,1)}, u32[]{:S(2)}, u32[]{:S(2)}) %collective-permute-start.10) | collective-permute-done | bytes 1310752 | tf_op jit(solution)/shard_map/ppermute | solution.py:80
  84.0 2.9 %collective-permute-start.14 = (bf16[352,4096]{1,0:T(8,128)(2,1)}, bf16[352,4096]{1,0:T(8,128)(2,1)}, u32[]{:S(2)}, u32[]{:S(2)}) collective-permute-start(bf16[352,4096]{1,0:T(8,128)(2,1)} %collective-permute-done.3.refs_1_), channel_id=1, source_target_pairs={{32,0},{33,1},{34,2},{35,3},{36,4},{37,5},{38,6},{39,7},{64,96},{6... | collective-permute-start | bytes 8650760 | tf_op jit(solution)/shard_map/ppermute | solution.py:80
  86.8 2.4 %collective-permute-start.15 = (bf16[160,4096]{1,0:T(8,128)(2,1)}, bf16[160,4096]{1,0:T(8,128)(2,1)}, u32[]{:S(2)}, u32[]{:S(2)}) collective-permute-start(bf16[160,4096]{1,0:T(8,128)(2,1)} %collective-permute-done.10.refs_2_), channel_id=1, source_target_pairs={{32,0},{33,1},{34,2},{35,3},{36,4},{37,5},{38,6},{39,7},{64,96},{6... | collective-permute-start | bytes 3932168 | tf_op jit(solution)/shard_map/ppermute | solution.py:80
  89.2 7.5 %shard_map.46.refs_20_ = f32[128,128]{1,0:T(8,128)} custom-call(s32[13]{0:T(128)} %stack.92.table, f32[4]{0:T(128)} %broadcast_select_fusion.4.factors, bf16[512,4096]{1,0:T(8,128)(2,1)} %refs_0_.1, bf16[352,4096]{1,0:T(8,128)(2,1)} %collective-permute-done.3.refs_1_, bf16[160,4096]{1,0:T(8,128)(2,1)} %collective-permute-done.10.refs_2_, ...), custom_call_target="tpu_custom_call" | custom-call | flops 2415919104 | bytes 9437184 | tf_op jit(solution)/shard_map/pallas_call | solution.py:203
  96.7 7.6 %shard_map.47 = f32[128,128]{1,0:T(8,128)} custom-call(s32[13]{0:T(128)} %stack.92.table, f32[4]{0:T(128)} %get-tuple-element.41.factors, bf16[352,4096]{1,0:T(8,128)(2,1)} %collective-permute-done.14.refs_0_, bf16[160,4096]{1,0:T(8,128)(2,1)} %collective-permute-done.15.refs_1_, bf16[512,4096]{1,0:T(8,128)(2,1)} %collective-permute-done.13.refs_2_, ...), custom_call_target="tpu_custom_call" | custom-call | flops 2415919104 | bytes 9437184 | tf_op jit(solution)/shard_map/pallas_call | solution.py:203
  104.3 15.4 %all_to_all.5 = f32[128,1,128]{2,1,0:T(1,128)S(1)} all-to-all(f32[128,1,128]{2,1,0:T(1,128)} %bitcast.26), channel_id=1, replica_groups=mesh['blk'=4,'ga'=32] {'blk','ga'}, dimensions={0} | all-to-all | bytes 131072 | tf_op jit(solution)/shard_map/all_to_all | solution.py:321
  (56 shorter events, 12.5 us)
Async XLA Ops:
  0.0 6.7 %copy-start.2 = (bf16[512,512]{1,0:T(8,128)(2,1)S(1)}, bf16[512,512]{1,0:T(8,128)(2,1)}, u32[]{:S(2)}) copy-start(bf16[512,512]{1,0:T(8,128)(2,1)} %refs_10_.3) | copy-start | bytes 1572868
  3.3 17.6 %collective-permute-start = (bf16[528,512]{1,0:T(8,128)(2,1)}, bf16[528,512]{1,0:T(8,128)(2,1)S(1)}, u32[]{:S(2)}, u32[]{:S(2)}) collective-permute-start(bf16[528,512]{1,0:T(8,128)(2,1)} %pad_maximum_fusion), channel_id=1, source_target_pairs={{0,24},{32,56},{1,25},{33,57},{2,26},{34,58},{3,27},{35,59},{4,28}... | collective-permute-start | bytes 1622024 | tf_op jit(solution)/shard_map/ppermute | solution.py:80
  6.7 12.6 %collective-permute-start.2 = (bf16[512,512]{1,0:T(8,128)(2,1)S(1)}, bf16[512,512]{1,0:T(8,128)(2,1)S(1)}, u32[]{:S(2)}, u32[]{:S(2)}) collective-permute-start(bf16[512,512]{1,0:T(8,128)(2,1)S(1)} %broadcast_multiply_fusion.refs_3_.refs_5_.refs_6_.refs_8_), channel_id=1, source_target_pairs={{0,8},{32,40},{1,9},{33,41},{2,10},{34,42},{3,11},{35,43},{4,12},{... | collective-permute-start | bytes 1572872 | tf_op jit(solution)/shard_map/ppermute | solution.py:80
  6.8 14.2 %collective-permute-start.1 = (bf16[512,512]{1,0:T(8,128)(2,1)S(1)}, bf16[512,512]{1,0:T(8,128)(2,1)S(1)}, u32[]{:S(2)}, u32[]{:S(2)}) collective-permute-start(bf16[512,512]{1,0:T(8,128)(2,1)S(1)} %copy-done.2), channel_id=1, source_target_pairs={{0,4},{32,36},{1,5},{33,37},{2,6},{34,38},{3,7},{35,39},{4,0},{36,... | collective-permute-start | bytes 1572872 | tf_op jit(solution)/shard_map/ppermute | solution.py:80
  19.3 27.0 %copy-start.3 = (bf16[512,512]{1,0:T(8,128)(2,1)}, bf16[512,512]{1,0:T(8,128)(2,1)S(1)}, u32[]{:S(2)}) copy-start(bf16[512,512]{1,0:T(8,128)(2,1)S(1)} %collective-permute-done.2.refs_6_.refs_8_.refs_3_.refs_5_) | copy-start | bytes 1572868
  21.0 6.7 %copy-start.6 = (bf16[512,512]{1,0:T(8,128)(2,1)}, bf16[512,512]{1,0:T(8,128)(2,1)S(1)}, u32[]{:S(2)}) copy-start(bf16[512,512]{1,0:T(8,128)(2,1)S(1)} %collective-permute-done.1.refs_12_) | copy-start | bytes 1572868
  21.0 26.7 %copy-start = (bf16[528,512]{1,0:T(8,128)(2,1)}, bf16[528,512]{1,0:T(8,128)(2,1)S(1)}, u32[]{:S(2)}) copy-start(bf16[528,512]{1,0:T(8,128)(2,1)S(1)} %collective-permute-done.refs_4_.refs_11_.refs_7_) | copy-start | bytes 1622020
  21.0 41.5 %collective-permute-start.3 = (bf16[352,4096]{1,0:T(8,128)(2,1)}, bf16[352,4096]{1,0:T(8,128)(2,1)}, u32[]{:S(2)}, u32[]{:S(2)}) collective-permute-start(bf16[352,4096]{1,0:T(8,128)(2,1)} %slice.16), channel_id=1, source_target_pairs={{32,8},{33,9},{34,10},{35,11},{36,12},{37,13},{38,14},{39,15},{64,... | collective-permute-start | bytes 8650760 | tf_op jit(solution)/shard_map/ppermute | solution.py:80
  26.3 13.8 %collective-permute-start.4 = (bf16[528,512]{1,0:T(8,128)(2,1)S(1)}, bf16[528,512]{1,0:T(8,128)(2,1)}, u32[]{:S(2)}, u32[]{:S(2)}) collective-permute-start(bf16[528,512]{1,0:T(8,128)(2,1)S(1)} %collective-permute-done.refs_4_.refs_11_.refs_7_), channel_id=1, source_target_pairs={{0,4},{32,36},{1,5},{33,37},{2,6},{34,38},{3,7},{35,39},{4,0},{36,... | collective-permute-start | bytes 1622024 | tf_op jit(solution)/shard_map/ppermute | solution.py:80
  27.7 12.4 %copy-start.7 = (bf16[512,512]{1,0:T(8,128)(2,1)S(1)}, bf16[512,512]{1,0:T(8,128)(2,1)}, u32[]{:S(2)}) copy-start(bf16[512,512]{1,0:T(8,128)(2,1)} %copy-done.6) | copy-start | bytes 1572868
  27.7 15.7 %collective-permute-start.6 = (bf16[528,512]{1,0:T(8,128)(2,1)S(1)}, bf16[528,512]{1,0:T(8,128)(2,1)S(1)}, u32[]{:S(2)}, u32[]{:S(2)}) collective-permute-start(bf16[528,512]{1,0:T(8,128)(2,1)S(1)} %collective-permute-done.refs_4_.refs_11_.refs_7_), channel_id=1, source_target_pairs={{0,1},{32,33},{1,2},{33,34},{2,3},{34,35},{3,0},{35,32},{4,5},{36,... | collective-permute-start | bytes 1622024 | tf_op jit(solution)/shard_map/ppermute | solution.py:80
  29.4 13.8 %collective-permute-start.5 = (bf16[512,512]{1,0:T(8,128)(2,1)S(1)}, bf16[512,512]{1,0:T(8,128)(2,1)S(1)}, u32[]{:S(2)}, u32[]{:S(2)}) collective-permute-start(bf16[512,512]{1,0:T(8,128)(2,1)S(1)} %multiply_add_fusion.2), channel_id=1, source_target_pairs={{0,3},{32,35},{1,0},{33,32},{2,1},{34,33},{3,2},{35,34},{4,7},{36,... | collective-permute-start | bytes 1572872 | tf_op jit(solution)/shard_map/ppermute | solution.py:80
  43.2 19.3 %copy-start.8 = (bf16[512,512]{1,0:T(8,128)(2,1)}, bf16[512,512]{1,0:T(8,128)(2,1)S(1)}, u32[]{:S(2)}) copy-start(bf16[512,512]{1,0:T(8,128)(2,1)S(1)} %collective-permute-done.5.refs_14_) | copy-start | bytes 1572868
  43.4 23.5 %copy-start.4 = (bf16[528,512]{1,0:T(8,128)(2,1)}, bf16[528,512]{1,0:T(8,128)(2,1)S(1)}, u32[]{:S(2)}) copy-start(bf16[528,512]{1,0:T(8,128)(2,1)S(1)} %collective-permute-done.6.refs_15_) | copy-start | bytes 1622020
  43.4 19.1 %collective-permute-start.9 = (bf16[528,512]{1,0:T(8,128)(2,1)}, bf16[528,512]{1,0:T(8,128)(2,1)S(1)}, u32[]{:S(2)}, u32[]{:S(2)}) collective-permute-start(bf16[528,512]{1,0:T(8,128)(2,1)} %collective-permute-done.4.refs_13_), channel_id=1, source_target_pairs={{0,1},{32,33},{1,2},{33,34},{2,3},{34,35},{3,0},{35,32},{4,5},{36,... | collective-permute-start | bytes 1622024 | tf_op jit(solution)/shard_map/ppermute | solution.py:80
  45.1 12.8 %collective-permute-start.8 = (bf16[512,512]{1,0:T(8,128)(2,1)S(1)}, bf16[512,512]{1,0:T(8,128)(2,1)S(1)}, u32[]{:S(2)}, u32[]{:S(2)}) collective-permute-start(bf16[512,512]{1,0:T(8,128)(2,1)S(1)} %fusion), channel_id=1, source_target_pairs={{0,3},{32,35},{1,0},{33,32},{2,1},{34,33},{3,2},{35,34},{4,7},{36,... | collective-permute-start | bytes 1572872 | tf_op jit(solution)/shard_map/ppermute | solution.py:80
  46.3 16.2 %collective-permute-start.7 = (bf16[512,512]{1,0:T(8,128)(2,1)S(1)}, bf16[512,512]{1,0:T(8,128)(2,1)S(1)}, u32[]{:S(2)}, u32[]{:S(2)}) collective-permute-start(bf16[512,512]{1,0:T(8,128)(2,1)S(1)} %collective-permute-done.2.refs_6_.refs_8_.refs_3_.refs_5_), channel_id=1, source_target_pairs={{64,0},{96,32},{65,1},{97,33},{66,2},{98,34},{67,3},{99,35},{68,4}... | collective-permute-start | bytes 1572872 | tf_op jit(solution)/shard_map/ppermute | solution.py:80
  63.3 20.7 %collective-permute-start.13 = (bf16[512,4096]{1,0:T(8,128)(2,1)}, bf16[512,4096]{1,0:T(8,128)(2,1)}, u32[]{:S(2)}, u32[]{:S(2)}) collective-permute-start(bf16[512,4096]{1,0:T(8,128)(2,1)} %refs_0_.1), channel_id=1, source_target_pairs={{0,32},{1,33},{2,34},{3,35},{4,36},{5,37},{6,38},{7,39},{96,64},{9... | collective-permute-start | bytes 12582920 | tf_op jit(solution)/shard_map/ppermute | solution.py:80
  64.7 19.2 %collective-permute-start.10 = (bf16[160,4096]{1,0:T(8,128)(2,1)}, bf16[160,4096]{1,0:T(8,128)(2,1)}, u32[]{:S(2)}, u32[]{:S(2)}) collective-permute-start(bf16[160,4096]{1,0:T(8,128)(2,1)} %slice.17), channel_id=1, source_target_pairs={{32,8},{33,9},{34,10},{35,11},{36,12},{37,13},{38,14},{39,15},{64,... | collective-permute-start | bytes 3932168 | tf_op jit(solution)/shard_map/ppermute | solution.py:80
  66.8 11.9 %collective-permute-start.12 = (bf16[528,512]{1,0:T(8,128)(2,1)S(1)}, bf16[528,512]{1,0:T(8,128)(2,1)}, u32[]{:S(2)}, u32[]{:S(2)}) collective-permute-start(bf16[528,512]{1,0:T(8,128)(2,1)S(1)} %multiply_add_fusion), channel_id=1, source_target_pairs={{0,1},{32,33},{1,2},{33,34},{2,3},{34,35},{3,0},{35,32},{4,5},{36,... | collective-permute-start | bytes 1622024 | tf_op jit(solution)/shard_map/ppermute | solution.py:80
  66.9 10.4 %collective-permute-start.11 = (bf16[512,512]{1,0:T(8,128)(2,1)S(1)}, bf16[512,512]{1,0:T(8,128)(2,1)S(1)}, u32[]{:S(2)}, u32[]{:S(2)}) collective-permute-start(bf16[512,512]{1,0:T(8,128)(2,1)S(1)} %multiply_add_fusion.1), channel_id=1, source_target_pairs={{0,3},{32,35},{1,0},{33,32},{2,1},{34,33},{3,2},{35,34},{4,7},{36,... | collective-permute-start | bytes 1572872 | tf_op jit(solution)/shard_map/ppermute | solution.py:80
  77.3 11.9 %copy-start.13 = (bf16[512,512]{1,0:T(8,128)(2,1)}, bf16[512,512]{1,0:T(8,128)(2,1)S(1)}, u32[]{:S(2)}) copy-start(bf16[512,512]{1,0:T(8,128)(2,1)S(1)} %collective-permute-done.11.refs_18_) | copy-start | bytes 1572868
  84.0 12.7 %collective-permute-start.14 = (bf16[352,4096]{1,0:T(8,128)(2,1)}, bf16[352,4096]{1,0:T(8,128)(2,1)}, u32[]{:S(2)}, u32[]{:S(2)}) collective-permute-start(bf16[352,4096]{1,0:T(8,128)(2,1)} %collective-permute-done.3.refs_1_), channel_id=1, source_target_pairs={{32,0},{33,1},{34,2},{35,3},{36,4},{37,5},{38,6},{39,7},{64,96},{6... | collective-permute-start | bytes 8650760 | tf_op jit(solution)/shard_map/ppermute | solution.py:80
  86.8 9.8 %collective-permute-start.15 = (bf16[160,4096]{1,0:T(8,128)(2,1)}, bf16[160,4096]{1,0:T(8,128)(2,1)}, u32[]{:S(2)}, u32[]{:S(2)}) collective-permute-start(bf16[160,4096]{1,0:T(8,128)(2,1)} %collective-permute-done.10.refs_2_), channel_id=1, source_target_pairs={{32,0},{33,1},{34,2},{35,3},{36,4},{37,5},{38,6},{39,7},{64,96},{6... | collective-permute-start | bytes 3932168 | tf_op jit(solution)/shard_map/ppermute | solution.py:80
  (6 other events, 23.8 us)
where the time goes:
time: 121 us; the launch traced here: 120 us
  waiting for transfers between devices  42.1 us (35%)
  starting transfers between devices  32.7 us (27%)
  blocking collectives  15.4 us (13%)
  Pallas kernels  15.1 us (12%)
  local copies, waits for them, and re-layouts  7.78 us (6%)
  other arithmetic  6.25 us (5%)
    ppermute x16, waiting for transfers between devices, send(): return lax.ppermute(value, AXES, table)  42.1 us
    ppermute x16, starting transfers between devices, send(): return lax.ppermute(value, AXES, table)  32.7 us
    all_to_all x1, blocking collectives, shards(): parts = lax.all_to_all(value.reshape(NS, 1, NS), AXES, 0, 0)  15.4 us
    pallas_call x2, Pallas kernels, products(): pl.pallas_call(kernel, out_shape=jax.ShapeDtypeStruct((NS, NS), jnp.float...  15.1 us
    slice x1, local copies, waits for them, and re-layouts, shards(): screening[:cut]  3.69 us
    slice x1, local copies, waits for them, and re-layouts, shards(): screening[cut:]  2.54 us
  transfers between devices with their start and end apart: 16, of which 10 were waited for; matrix products, arithmetic and copies ran while one was open for 8% of the time, Pallas kernels for 6%

commit v1 on v0

--- a/solution.py
+++ b/solution.py
@@ -145,6 +145,8 @@
             else:
                 choose(flag, [(yes, target, sem)], [(no, target, sem)])
             columns = pl.ds(pl.multiple_of(table[slot] * depth, depth), depth)
+            if slot == 4:
+                continue
             copies = []
             for side in (near_refs, far_refs):
                 at, triples = 0, []
@@ -173,9 +175,14 @@
         result = jnp.zeros((NS, 2 * NS), jnp.float32)
         for group in range(2):
             wait(q.at[group], sems.at[0, group])
-            wait(w.at[group], sems.at[1, group])
+            rest = pl.ds(group * depth, (4 - group) * depth)
+            wait(w.at[group, :, rest], sems.at[1, group])
             q[group, :depth] = q[group, :depth] * factors[group].astype(q.dtype)
-            total = jnp.dot(w[group], q[group], preferred_element_type=jnp.float32)
+            total = jnp.dot(w[group, :, rest], q[group, rest], preferred_element_type=jnp.float32)
+            if group == 1:
+                total = total + jnp.dot(
+                    w[0, :, :depth], q[group, :depth], preferred_element_type=jnp.float32
+                )
             total = total + side * factors[2 + group]
             if group == 1:
                 total = total * weight_ref[0:1, :].astype(jnp.float32)

time: 121 us -> 121 us (level)
  no operation moved by 1% of the time
where the time goes in v1:
time: 121 us; the launch traced here: 120 us
  waiting for transfers between devices  42.1 us (35%)
  starting transfers between devices  32.7 us (27%)
  blocking collectives  15.4 us (13%)
  Pallas kernels  14.8 us (12%)
  local copies, waits for them, and re-layouts  7.78 us (6%)
  other arithmetic  6.25 us (5%)
    ppermute x16, waiting for transfers between devices, send(): return lax.ppermute(value, AXES, table)  42.1 us
    ppermute x16, starting transfers between devices, send(): return lax.ppermute(value, AXES, table)  32.7 us
    all_to_all x1, blocking collectives, shards(): parts = lax.all_to_all(value.reshape(NS, 1, NS), AXES, 0, 0)  15.4 us
    pallas_call x2, Pallas kernels, products(): pl.pallas_call(kernel, out_shape=jax.ShapeDtypeStruct((NS, NS), jnp.float...  14.8 us
    slice x1, local copies, waits for them, and re-layouts, shards(): screening[:cut]  3.69 us
    slice x1, local copies, waits for them, and re-layouts, shards(): screening[cut:]  2.54 us
  transfers between devices with their start and end apart: 16, of which 10 were waited for; matrix products, arithmetic and copies ran while one was open for 8% of the time, Pallas kernels for 6%

profile of v1, /device:TPU:1, one launch (start us, length us, event | category | flops | bytes accessed | tf_op | source)
XLA Modules:
  0.0 120.1 jit_solution(12550738520981148419)
XLA Ops:
  1.5 1.9 %pad_maximum_fusion = bf16[528,512]{1,0:T(8,128)(2,1)} fusion(bf16[16,512]{1,0:T(8,128)(2,1)S(1)} %broadcast_in_dim.25, bf16[512,512]{1,0:T(8,128)(2,1)} %refs_10_.3), kind=kLoop, calls=%fused_computation | loop fusion | flops 1081344 | bytes 1081344 | tf_op jit(solution)/shard_map/concatenate | solution.py:266
  3.3 3.3 %collective-permute-start = (bf16[528,512]{1,0:T(8,128)(2,1)}, bf16[528,512]{1,0:T(8,128)(2,1)S(1)}, u32[]{:S(2)}, u32[]{:S(2)}) collective-permute-start(bf16[528,512]{1,0:T(8,128)(2,1)} %pad_maximum_fusion), channel_id=1, source_target_pairs={{0,24},{32,56},{1,25},{33,57},{2,26},{34,58},{3,27},{35,59},{4,28}... | collective-permute-start | bytes 1622024 | tf_op jit(solution)/shard_map/ppermute | solution.py:80
  6.8 3.2 %collective-permute-start.1 = (bf16[512,512]{1,0:T(8,128)(2,1)S(1)}, bf16[512,512]{1,0:T(8,128)(2,1)S(1)}, u32[]{:S(2)}, u32[]{:S(2)}) collective-permute-start(bf16[512,512]{1,0:T(8,128)(2,1)S(1)} %copy-done.2), channel_id=1, source_target_pairs={{0,4},{32,36},{1,5},{33,37},{2,6},{34,38},{3,7},{35,39},{4,0},{36,... | collective-permute-start | bytes 1572872 | tf_op jit(solution)/shard_map/ppermute | solution.py:80
  10.2 2.5 %slice.17 = bf16[160,4096]{1,0:T(8,128)(2,1)} slice(bf16[512,4096]{1,0:T(8,128)(2,1)} %refs_0_.1), slice={[352:512], [0:4096]} | slice | bytes 2621440 | tf_op jit(solution)/shard_map/slice | solution.py:275
  12.7 3.7 %slice.16 = bf16[352,4096]{1,0:T(8,128)(2,1)} slice(bf16[512,4096]{1,0:T(8,128)(2,1)} %refs_0_.1), slice={[0:352], [0:4096]} | slice | bytes 5767168 | tf_op jit(solution)/shard_map/slice | solution.py:275
  19.3 1.7 %collective-permute-done.1.refs_12_ = bf16[512,512]{1,0:T(8,128)(2,1)S(1)} collective-permute-done((bf16[512,512]{1,0:T(8,128)(2,1)S(1)}, bf16[512,512]{1,0:T(8,128)(2,1)S(1)}, u32[]{:S(2)}, u32[]{:S(2)}) %collective-permute-start.1) | collective-permute-done | bytes 524320 | tf_op jit(solution)/shard_map/ppermute | solution.py:80
  21.0 5.3 %collective-permute-start.3 = (bf16[352,4096]{1,0:T(8,128)(2,1)}, bf16[352,4096]{1,0:T(8,128)(2,1)}, u32[]{:S(2)}, u32[]{:S(2)}) collective-permute-start(bf16[352,4096]{1,0:T(8,128)(2,1)} %slice.16), channel_id=1, source_target_pairs={{32,8},{33,9},{34,10},{35,11},{36,12},{37,13},{38,14},{39,15},{64,... | collective-permute-start | bytes 8650760 | tf_op jit(solution)/shard_map/ppermute | solution.py:80
  27.7 1.6 %collective-permute-start.6 = (bf16[528,512]{1,0:T(8,128)(2,1)S(1)}, bf16[528,512]{1,0:T(8,128)(2,1)S(1)}, u32[]{:S(2)}, u32[]{:S(2)}) collective-permute-start(bf16[528,512]{1,0:T(8,128)(2,1)S(1)} %collective-permute-done.refs_4_.refs_11_.refs_7_), channel_id=1, source_target_pairs={{0,1},{32,33},{1,2},{33,34},{2,3},{34,35},{3,0},{35,32},{4,5},{36,... | collective-permute-start | bytes 1622024 | tf_op jit(solution)/shard_map/ppermute | solution.py:80
  29.4 2.2 %collective-permute-start.5 = (bf16[512,512]{1,0:T(8,128)(2,1)S(1)}, bf16[512,512]{1,0:T(8,128)(2,1)S(1)}, u32[]{:S(2)}, u32[]{:S(2)}) collective-permute-start(bf16[512,512]{1,0:T(8,128)(2,1)S(1)} %multiply_add_fusion.2), channel_id=1, source_target_pairs={{0,3},{32,35},{1,0},{33,32},{2,1},{34,33},{3,2},{35,34},{4,7},{36,... | collective-permute-start | bytes 1572872 | tf_op jit(solution)/shard_map/ppermute | solution.py:80
  31.6 8.5 %collective-permute-done.4.refs_13_ = bf16[528,512]{1,0:T(8,128)(2,1)} collective-permute-done((bf16[528,512]{1,0:T(8,128)(2,1)S(1)}, bf16[528,512]{1,0:T(8,128)(2,1)}, u32[]{:S(2)}, u32[]{:S(2)}) %collective-permute-start.4) | collective-permute-done | bytes 540704 | tf_op jit(solution)/shard_map/ppermute | solution.py:80
  41.2 2.0 %collective-permute-done.5.refs_14_ = bf16[512,512]{1,0:T(8,128)(2,1)S(1)} collective-permute-done((bf16[512,512]{1,0:T(8,128)(2,1)S(1)}, bf16[512,512]{1,0:T(8,128)(2,1)S(1)}, u32[]{:S(2)}, u32[]{:S(2)}) %collective-permute-start.5) | collective-permute-done | bytes 524320 | tf_op jit(solution)/shard_map/ppermute | solution.py:80
  43.4 1.7 %collective-permute-start.9 = (bf16[528,512]{1,0:T(8,128)(2,1)}, bf16[528,512]{1,0:T(8,128)(2,1)S(1)}, u32[]{:S(2)}, u32[]{:S(2)}) collective-permute-start(bf16[528,512]{1,0:T(8,128)(2,1)} %collective-permute-done.4.refs_13_), channel_id=1, source_target_pairs={{0,1},{32,33},{1,2},{33,34},{2,3},{34,35},{3,0},{35,32},{4,5},{36,... | collective-permute-start | bytes 1622024 | tf_op jit(solution)/shard_map/ppermute | solution.py:80
  48.2 9.6 %collective-permute-done.8.refs_16_ = bf16[512,512]{1,0:T(8,128)(2,1)S(1)} collective-permute-done((bf16[512,512]{1,0:T(8,128)(2,1)S(1)}, bf16[512,512]{1,0:T(8,128)(2,1)S(1)}, u32[]{:S(2)}, u32[]{:S(2)}) %collective-permute-start.8) | collective-permute-done | bytes 524320 | tf_op jit(solution)/shard_map/ppermute | solution.py:80
  57.9 4.6 %collective-permute-done.7.refs_7_.refs_4_ = bf16[512,512]{1,0:T(8,128)(2,1)S(1)} collective-permute-done((bf16[512,512]{1,0:T(8,128)(2,1)S(1)}, bf16[512,512]{1,0:T(8,128)(2,1)S(1)}, u32[]{:S(2)}, u32[]{:S(2)}) %collective-permute-start.7) | collective-permute-done | bytes 524320 | tf_op jit(solution)/shard_map/ppermute | solution.py:80
  63.3 1.4 %collective-permute-start.13 = (bf16[512,4096]{1,0:T(8,128)(2,1)}, bf16[512,4096]{1,0:T(8,128)(2,1)}, u32[]{:S(2)}, u32[]{:S(2)}) collective-permute-start(bf16[512,4096]{1,0:T(8,128)(2,1)} %refs_0_.1), channel_id=1, source_target_pairs={{0,32},{1,33},{2,34},{3,35},{4,36},{5,37},{6,38},{7,39},{96,64},{9... | collective-permute-start | bytes 12582920 | tf_op jit(solution)/shard_map/ppermute | solution.py:80
  64.7 1.9 %collective-permute-start.10 = (bf16[160,4096]{1,0:T(8,128)(2,1)}, bf16[160,4096]{1,0:T(8,128)(2,1)}, u32[]{:S(2)}, u32[]{:S(2)}) collective-permute-start(bf16[160,4096]{1,0:T(8,128)(2,1)} %slice.17), channel_id=1, source_target_pairs={{32,8},{33,9},{34,10},{35,11},{36,12},{37,13},{38,14},{39,15},{64,... | collective-permute-start | bytes 3932168 | tf_op jit(solution)/shard_map/ppermute | solution.py:80
  66.9 2.7 %collective-permute-start.11 = (bf16[512,512]{1,0:T(8,128)(2,1)S(1)}, bf16[512,512]{1,0:T(8,128)(2,1)S(1)}, u32[]{:S(2)}, u32[]{:S(2)}) collective-permute-start(bf16[512,512]{1,0:T(8,128)(2,1)S(1)} %multiply_add_fusion.1), channel_id=1, source_target_pairs={{0,3},{32,35},{1,0},{33,32},{2,1},{34,33},{3,2},{35,34},{4,7},{36,... | collective-permute-start | bytes 1572872 | tf_op jit(solution)/shard_map/ppermute | solution.py:80
  69.7 7.6 %collective-permute-done.11.refs_18_ = bf16[512,512]{1,0:T(8,128)(2,1)S(1)} collective-permute-done((bf16[512,512]{1,0:T(8,128)(2,1)S(1)}, bf16[512,512]{1,0:T(8,128)(2,1)S(1)}, u32[]{:S(2)}, u32[]{:S(2)}) %collective-permute-start.11) | collective-permute-done | bytes 524320 | tf_op jit(solution)/shard_map/ppermute | solution.py:80
  78.6 5.3 %collective-permute-done.10.refs_2_ = bf16[160,4096]{1,0:T(8,128)(2,1)} collective-permute-done((bf16[160,4096]{1,0:T(8,128)(2,1)}, bf16[160,4096]{1,0:T(8,128)(2,1)}, u32[]{:S(2)}, u32[]{:S(2)}) %collective-permute-start.10) | collective-permute-done | bytes 1310752 | tf_op jit(solution)/shard_map/ppermute | solution.py:80
  84.0 2.9 %collective-permute-start.14 = (bf16[352,4096]{1,0:T(8,128)(2,1)}, bf16[352,4096]{1,0:T(8,128)(2,1)}, u32[]{:S(2)}, u32[]{:S(2)}) collective-permute-start(bf16[352,4096]{1,0:T(8,128)(2,1)} %collective-permute-done.3.refs_1_), channel_id=1, source_target_pairs={{32,0},{33,1},{34,2},{35,3},{36,4},{37,5},{38,6},{39,7},{64,96},{6... | collective-permute-start | bytes 8650760 | tf_op jit(solution)/shard_map/ppermute | solution.py:80
  86.8 2.4 %collective-permute-start.15 = (bf16[160,4096]{1,0:T(8,128)(2,1)}, bf16[160,4096]{1,0:T(8,128)(2,1)}, u32[]{:S(2)}, u32[]{:S(2)}) collective-permute-start(bf16[160,4096]{1,0:T(8,128)(2,1)} %collective-permute-done.10.refs_2_), channel_id=1, source_target_pairs={{32,0},{33,1},{34,2},{35,3},{36,4},{37,5},{38,6},{39,7},{64,96},{6... | collective-permute-start | bytes 3932168 | tf_op jit(solution)/shard_map/ppermute | solution.py:80
  89.2 7.3 %shard_map.46.refs_20_ = f32[128,128]{1,0:T(8,128)} custom-call(s32[13]{0:T(128)} %stack.92.table, f32[4]{0:T(128)} %broadcast_select_fusion.4.factors, bf16[512,4096]{1,0:T(8,128)(2,1)} %refs_0_.1, bf16[352,4096]{1,0:T(8,128)(2,1)} %collective-permute-done.3.refs_1_, bf16[160,4096]{1,0:T(8,128)(2,1)} %collective-permute-done.10.refs_2_, ...), custom_call_target="tpu_custom_call" | custom-call | flops 2415919104 | bytes 9437184 | tf_op jit(solution)/shard_map/pallas_call | solution.py:210
  96.6 7.5 %shard_map.47 = f32[128,128]{1,0:T(8,128)} custom-call(s32[13]{0:T(128)} %stack.92.table, f32[4]{0:T(128)} %get-tuple-element.41.factors, bf16[352,4096]{1,0:T(8,128)(2,1)} %collective-permute-done.14.refs_0_, bf16[160,4096]{1,0:T(8,128)(2,1)} %collective-permute-done.15.refs_1_, bf16[512,4096]{1,0:T(8,128)(2,1)} %collective-permute-done.13.refs_2_, ...), custom_call_target="tpu_custom_call" | custom-call | flops 2415919104 | bytes 9437184 | tf_op jit(solution)/shard_map/pallas_call | solution.py:210
  104.1 15.4 %all_to_all.5 = f32[128,1,128]{2,1,0:T(1,128)S(1)} all-to-all(f32[128,1,128]{2,1,0:T(1,128)} %bitcast.26), channel_id=1, replica_groups=mesh['blk'=4,'ga'=32] {'blk','ga'}, dimensions={0} | all-to-all | bytes 131072 | tf_op jit(solution)/shard_map/all_to_all | solution.py:328
  (56 shorter events, 12.5 us)
Async XLA Ops:
  0.0 6.7 %copy-start.2 = (bf16[512,512]{1,0:T(8,128)(2,1)S(1)}, bf16[512,512]{1,0:T(8,128)(2,1)}, u32[]{:S(2)}) copy-start(bf16[512,512]{1,0:T(8,128)(2,1)} %refs_10_.3) | copy-start | bytes 1572868
  3.3 17.6 %collective-permute-start = (bf16[528,512]{1,0:T(8,128)(2,1)}, bf16[528,512]{1,0:T(8,128)(2,1)S(1)}, u32[]{:S(2)}, u32[]{:S(2)}) collective-permute-start(bf16[528,512]{1,0:T(8,128)(2,1)} %pad_maximum_fusion), channel_id=1, source_target_pairs={{0,24},{32,56},{1,25},{33,57},{2,26},{34,58},{3,27},{35,59},{4,28}... | collective-permute-start | bytes 1622024 | tf_op jit(solution)/shard_map/ppermute | solution.py:80
  6.7 12.6 %collective-permute-start.2 = (bf16[512,512]{1,0:T(8,128)(2,1)S(1)}, bf16[512,512]{1,0:T(8,128)(2,1)S(1)}, u32[]{:S(2)}, u32[]{:S(2)}) collective-permute-start(bf16[512,512]{1,0:T(8,128)(2,1)S(1)} %broadcast_multiply_fusion.refs_3_.refs_5_.refs_6_.refs_8_), channel_id=1, source_target_pairs={{0,8},{32,40},{1,9},{33,41},{2,10},{34,42},{3,11},{35,43},{4,12},{... | collective-permute-start | bytes 1572872 | tf_op jit(solution)/shard_map/ppermute | solution.py:80
  6.8 14.2 %collective-permute-start.1 = (bf16[512,512]{1,0:T(8,128)(2,1)S(1)}, bf16[512,512]{1,0:T(8,128)(2,1)S(1)}, u32[]{:S(2)}, u32[]{:S(2)}) collective-permute-start(bf16[512,512]{1,0:T(8,128)(2,1)S(1)} %copy-done.2), channel_id=1, source_target_pairs={{0,4},{32,36},{1,5},{33,37},{2,6},{34,38},{3,7},{35,39},{4,0},{36,... | collective-permute-start | bytes 1572872 | tf_op jit(solution)/shard_map/ppermute | solution.py:80
  19.3 27.0 %copy-start.3 = (bf16[512,512]{1,0:T(8,128)(2,1)}, bf16[512,512]{1,0:T(8,128)(2,1)S(1)}, u32[]{:S(2)}) copy-start(bf16[512,512]{1,0:T(8,128)(2,1)S(1)} %collective-permute-done.2.refs_6_.refs_8_.refs_3_.refs_5_) | copy-start | bytes 1572868
  21.0 6.7 %copy-start.6 = (bf16[512,512]{1,0:T(8,128)(2,1)}, bf16[512,512]{1,0:T(8,128)(2,1)S(1)}, u32[]{:S(2)}) copy-start(bf16[512,512]{1,0:T(8,128)(2,1)S(1)} %collective-permute-done.1.refs_12_) | copy-start | bytes 1572868
  21.0 26.7 %copy-start = (bf16[528,512]{1,0:T(8,128)(2,1)}, bf16[528,512]{1,0:T(8,128)(2,1)S(1)}, u32[]{:S(2)}) copy-start(bf16[528,512]{1,0:T(8,128)(2,1)S(1)} %collective-permute-done.refs_4_.refs_11_.refs_7_) | copy-start | bytes 1622020
  21.0 41.5 %collective-permute-start.3 = (bf16[352,4096]{1,0:T(8,128)(2,1)}, bf16[352,4096]{1,0:T(8,128)(2,1)}, u32[]{:S(2)}, u32[]{:S(2)}) collective-permute-start(bf16[352,4096]{1,0:T(8,128)(2,1)} %slice.16), channel_id=1, source_target_pairs={{32,8},{33,9},{34,10},{35,11},{36,12},{37,13},{38,14},{39,15},{64,... | collective-permute-start | bytes 8650760 | tf_op jit(solution)/shard_map/ppermute | solution.py:80
  26.3 13.8 %collective-permute-start.4 = (bf16[528,512]{1,0:T(8,128)(2,1)S(1)}, bf16[528,512]{1,0:T(8,128)(2,1)}, u32[]{:S(2)}, u32[]{:S(2)}) collective-permute-start(bf16[528,512]{1,0:T(8,128)(2,1)S(1)} %collective-permute-done.refs_4_.refs_11_.refs_7_), channel_id=1, source_target_pairs={{0,4},{32,36},{1,5},{33,37},{2,6},{34,38},{3,7},{35,39},{4,0},{36,... | collective-permute-start | bytes 1622024 | tf_op jit(solution)/shard_map/ppermute | solution.py:80
  27.7 12.4 %copy-start.7 = (bf16[512,512]{1,0:T(8,128)(2,1)S(1)}, bf16[512,512]{1,0:T(8,128)(2,1)}, u32[]{:S(2)}) copy-start(bf16[512,512]{1,0:T(8,128)(2,1)} %copy-done.6) | copy-start | bytes 1572868
  27.7 15.7 %collective-permute-start.6 = (bf16[528,512]{1,0:T(8,128)(2,1)S(1)}, bf16[528,512]{1,0:T(8,128)(2,1)S(1)}, u32[]{:S(2)}, u32[]{:S(2)}) collective-permute-start(bf16[528,512]{1,0:T(8,128)(2,1)S(1)} %collective-permute-done.refs_4_.refs_11_.refs_7_), channel_id=1, source_target_pairs={{0,1},{32,33},{1,2},{33,34},{2,3},{34,35},{3,0},{35,32},{4,5},{36,... | collective-permute-start | bytes 1622024 | tf_op jit(solution)/shard_map/ppermute | solution.py:80
  29.4 13.8 %collective-permute-start.5 = (bf16[512,512]{1,0:T(8,128)(2,1)S(1)}, bf16[512,512]{1,0:T(8,128)(2,1)S(1)}, u32[]{:S(2)}, u32[]{:S(2)}) collective-permute-start(bf16[512,512]{1,0:T(8,128)(2,1)S(1)} %multiply_add_fusion.2), channel_id=1, source_target_pairs={{0,3},{32,35},{1,0},{33,32},{2,1},{34,33},{3,2},{35,34},{4,7},{36,... | collective-permute-start | bytes 1572872 | tf_op jit(solution)/shard_map/ppermute | solution.py:80
  43.2 19.3 %copy-start.8 = (bf16[512,512]{1,0:T(8,128)(2,1)}, bf16[512,512]{1,0:T(8,128)(2,1)S(1)}, u32[]{:S(2)}) copy-start(bf16[512,512]{1,0:T(8,128)(2,1)S(1)} %collective-permute-done.5.refs_14_) | copy-start | bytes 1572868
  43.4 23.5 %copy-start.4 = (bf16[528,512]{1,0:T(8,128)(2,1)}, bf16[528,512]{1,0:T(8,128)(2,1)S(1)}, u32[]{:S(2)}) copy-start(bf16[528,512]{1,0:T(8,128)(2,1)S(1)} %collective-permute-done.6.refs_15_) | copy-start | bytes 1622020
  43.4 19.1 %collective-permute-start.9 = (bf16[528,512]{1,0:T(8,128)(2,1)}, bf16[528,512]{1,0:T(8,128)(2,1)S(1)}, u32[]{:S(2)}, u32[]{:S(2)}) collective-permute-start(bf16[528,512]{1,0:T(8,128)(2,1)} %collective-permute-done.4.refs_13_), channel_id=1, source_target_pairs={{0,1},{32,33},{1,2},{33,34},{2,3},{34,35},{3,0},{35,32},{4,5},{36,... | collective-permute-start | bytes 1622024 | tf_op jit(solution)/shard_map/ppermute | solution.py:80
  45.1 12.8 %collective-permute-start.8 = (bf16[512,512]{1,0:T(8,128)(2,1)S(1)}, bf16[512,512]{1,0:T(8,128)(2,1)S(1)}, u32[]{:S(2)}, u32[]{:S(2)}) collective-permute-start(bf16[512,512]{1,0:T(8,128)(2,1)S(1)} %fusion), channel_id=1, source_target_pairs={{0,3},{32,35},{1,0},{33,32},{2,1},{34,33},{3,2},{35,34},{4,7},{36,... | collective-permute-start | bytes 1572872 | tf_op jit(solution)/shard_map/ppermute | solution.py:80
  46.3 16.2 %collective-permute-start.7 = (bf16[512,512]{1,0:T(8,128)(2,1)S(1)}, bf16[512,512]{1,0:T(8,128)(2,1)S(1)}, u32[]{:S(2)}, u32[]{:S(2)}) collective-permute-start(bf16[512,512]{1,0:T(8,128)(2,1)S(1)} %collective-permute-done.2.refs_6_.refs_8_.refs_3_.refs_5_), channel_id=1, source_target_pairs={{64,0},{96,32},{65,1},{97,33},{66,2},{98,34},{67,3},{99,35},{68,4}... | collective-permute-start | bytes 1572872 | tf_op jit(solution)/shard_map/ppermute | solution.py:80
  63.3 20.7 %collective-permute-start.13 = (bf16[512,4096]{1,0:T(8,128)(2,1)}, bf16[512,4096]{1,0:T(8,128)(2,1)}, u32[]{:S(2)}, u32[]{:S(2)}) collective-permute-start(bf16[512,4096]{1,0:T(8,128)(2,1)} %refs_0_.1), channel_id=1, source_target_pairs={{0,32},{1,33},{2,34},{3,35},{4,36},{5,37},{6,38},{7,39},{96,64},{9... | collective-permute-start | bytes 12582920 | tf_op jit(solution)/shard_map/ppermute | solution.py:80
  64.7 19.2 %collective-permute-start.10 = (bf16[160,4096]{1,0:T(8,128)(2,1)}, bf16[160,4096]{1,0:T(8,128)(2,1)}, u32[]{:S(2)}, u32[]{:S(2)}) collective-permute-start(bf16[160,4096]{1,0:T(8,128)(2,1)} %slice.17), channel_id=1, source_target_pairs={{32,8},{33,9},{34,10},{35,11},{36,12},{37,13},{38,14},{39,15},{64,... | collective-permute-start | bytes 3932168 | tf_op jit(solution)/shard_map/ppermute | solution.py:80
  66.8 11.9 %collective-permute-start.12 = (bf16[528,512]{1,0:T(8,128)(2,1)S(1)}, bf16[528,512]{1,0:T(8,128)(2,1)}, u32[]{:S(2)}, u32[]{:S(2)}) collective-permute-start(bf16[528,512]{1,0:T(8,128)(2,1)S(1)} %multiply_add_fusion), channel_id=1, source_target_pairs={{0,1},{32,33},{1,2},{33,34},{2,3},{34,35},{3,0},{35,32},{4,5},{36,... | collective-permute-start | bytes 1622024 | tf_op jit(solution)/shard_map/ppermute | solution.py:80
  66.9 10.4 %collective-permute-start.11 = (bf16[512,512]{1,0:T(8,128)(2,1)S(1)}, bf16[512,512]{1,0:T(8,128)(2,1)S(1)}, u32[]{:S(2)}, u32[]{:S(2)}) collective-permute-start(bf16[512,512]{1,0:T(8,128)(2,1)S(1)} %multiply_add_fusion.1), channel_id=1, source_target_pairs={{0,3},{32,35},{1,0},{33,32},{2,1},{34,33},{3,2},{35,34},{4,7},{36,... | collective-permute-start | bytes 1572872 | tf_op jit(solution)/shard_map/ppermute | solution.py:80
  77.3 11.9 %copy-start.13 = (bf16[512,512]{1,0:T(8,128)(2,1)}, bf16[512,512]{1,0:T(8,128)(2,1)S(1)}, u32[]{:S(2)}) copy-start(bf16[512,512]{1,0:T(8,128)(2,1)S(1)} %collective-permute-done.11.refs_18_) | copy-start | bytes 1572868
  84.0 12.6 %collective-permute-start.14 = (bf16[352,4096]{1,0:T(8,128)(2,1)}, bf16[352,4096]{1,0:T(8,128)(2,1)}, u32[]{:S(2)}, u32[]{:S(2)}) collective-permute-start(bf16[352,4096]{1,0:T(8,128)(2,1)} %collective-permute-done.3.refs_1_), channel_id=1, source_target_pairs={{32,0},{33,1},{34,2},{35,3},{36,4},{37,5},{38,6},{39,7},{64,96},{6... | collective-permute-start | bytes 8650760 | tf_op jit(solution)/shard_map/ppermute | solution.py:80
  86.8 9.7 %collective-permute-start.15 = (bf16[160,4096]{1,0:T(8,128)(2,1)}, bf16[160,4096]{1,0:T(8,128)(2,1)}, u32[]{:S(2)}, u32[]{:S(2)}) collective-permute-start(bf16[160,4096]{1,0:T(8,128)(2,1)} %collective-permute-done.10.refs_2_), channel_id=1, source_target_pairs={{32,0},{33,1},{34,2},{35,3},{36,4},{37,5},{38,6},{39,7},{64,96},{6... | collective-permute-start | bytes 3932168 | tf_op jit(solution)/shard_map/ppermute | solution.py:80
  (6 other events, 23.8 us)
